TPU v7x, 256 devices: a whole 4x4x8 slice. The times are simulated.
256 devices in a mesh: dp: 16 (over x, y), expert: 16 (over z, core).
Axes of the slice: x: 4, y: 4, z: 8, core: 2. Of those that a mesh axis runs over, the one named last changes fastest.
Arguments:
- tokens: bfloat16 [40960, 2048], P(('dp', 'expert')), may hold values from -6 to 6
- routes: int32 [40960, 2], P(('dp', 'expert')), may hold values from 0 to 15, all different within a row; in each aligned block of 160 rows (0 to 159, 160 to 319, ...) at most 30 rows name the same one
- route_gains: float32 [40960, 2], P(('dp', 'expert')), may hold values from 0.1 to 1
- cotangent: bfloat16 [40960, 2048], P(('dp', 'expert')), may hold values from -24 to 24
- w_gate: bfloat16 [16, 2048, 768], P('expert'), may hold values from -0.125 to 0.125
- w_up: bfloat16 [16, 2048, 768], P('expert'), may hold values from -0.125 to 0.125
- w_down: bfloat16 [16, 2048, 768], P('expert'), may hold values from -0.21875 to 0.21875
Outputs:
- layer_output: bfloat16 [40960, 2048], P(('dp', 'expert'))
- input_grad: bfloat16 [40960, 2048], P(('dp', 'expert'))
- grad_gate: bfloat16 [16, 2048, 768], P('expert', 'dp')
- grad_up: bfloat16 [16, 2048, 768], P('expert', 'dp')
- grad_down: bfloat16 [16, 2048, 768], P('expert', 'dp')
Inputs may be any that keep to these rules, and one draw needn't show every extreme that they name: `routes`: each row names 2 different experts. Within the rows of one device (aligned blocks of 160 rows) no expert is named more than 30 times, and in some device's rows one expert is named exactly 30 times.
All inputs are finite; a program needn't handle non-finite values.
Results may differ from a plain program's by a relative error of at most 0.015.
Values may be sent and summed in bfloat16 or wider, within the bound.
A program may use at most 128 MiB of HBM per device.

v0:
```python
import jax
import jax.numpy as jnp
from jax import lax
from jax.sharding import PartitionSpec as P

SLOTS = 32


def slot_masks(routes, experts):
    rows, picks = routes.shape
    chosen = routes.T.reshape(1, -1)
    labels = lax.broadcasted_iota(jnp.int32, (experts, rows * picks), 0)
    matches = chosen == labels
    total = rows * picks
    earlier = lax.broadcasted_iota(jnp.int32, (total, total), 0) < lax.broadcasted_iota(
        jnp.int32, (total, total), 1
    )
    before = jnp.dot(
        matches.astype(jnp.bfloat16),
        earlier.astype(jnp.bfloat16),
        preferred_element_type=jnp.float32,
    )
    position = jnp.sum(jnp.where(matches, before, 0.0), axis=0).astype(jnp.int32)
    target = chosen[0] * SLOTS + position
    slots = lax.broadcasted_iota(jnp.int32, (experts * SLOTS, total), 0)
    return (slots == target[None, :]).reshape(experts * SLOTS, picks, rows)


def rows_t(left, right):
    return lax.dot_general(
        left, right, (((1,), (1,)), ((), ())), preferred_element_type=jnp.float32
    )


def outer_rows(left, right):
    return lax.dot_general(
        left, right, (((0,), (0,)), ((), ())), preferred_element_type=jnp.float32
    )


def shards(tokens, routes, route_gains, cotangent, w_gate, w_up, w_down):
    experts = lax.axis_size("expert")
    groups = lax.axis_size("dp")
    width = tokens.shape[1]
    depth = width // groups
    flip = [(a * experts + b, b * experts + a) for a in range(groups) for b in range(experts)]
    mine = lax.axis_index("dp") * depth
    hidden_units = w_gate.shape[2]

    def fetch(w):
        part = lax.dynamic_slice_in_dim(w[0], mine, depth, axis=0)
        return part

    part = jnp.concatenate([fetch(w_gate), fetch(w_up), fetch(w_down)], axis=1)
    part = lax.ppermute(part, ("dp", "expert"), flip)
    full = lax.all_gather(part, "expert", axis=0, tiled=True)
    gate_mat = full[:, :hidden_units]
    up_mat = full[:, hidden_units : 2 * hidden_units]
    down_mat = full[:, 2 * hidden_units :]
    masks = slot_masks(routes, groups)
    first = masks[:, 0, :].astype(jnp.bfloat16)
    second = masks[:, 1, :].astype(jnp.bfloat16)
    both = first + second
    gains = route_gains.T
    slot_gain = jnp.sum(jnp.where(masks, gains[None], 0.0), axis=(1, 2))
    send_tok = jnp.dot(both, tokens, preferred_element_type=jnp.float32).astype(jnp.bfloat16)
    send_cot = (
        slot_gain[:, None] * jnp.dot(both, cotangent, preferred_element_type=jnp.float32)
    ).astype(jnp.bfloat16)

    def exchange(block):
        block = block.reshape(groups, SLOTS, width)
        block = lax.all_to_all(block, "dp", split_axis=0, concat_axis=0, tiled=True)
        return block.reshape(groups * SLOTS, width)

    arrived = exchange(send_tok)
    arrived_cot = exchange(send_cot)
    pre_gate = jnp.dot(arrived, gate_mat, preferred_element_type=jnp.float32)
    pre_up = jnp.dot(arrived, up_mat, preferred_element_type=jnp.float32)
    sigma = jax.nn.sigmoid(pre_gate)
    activated = pre_gate * sigma
    hidden = (activated * pre_up).astype(jnp.bfloat16)
    d_hidden = jnp.dot(arrived_cot, down_mat, preferred_element_type=jnp.float32)
    d_gate = (d_hidden * pre_up * (sigma * (1.0 + pre_gate * (1.0 - sigma)))).astype(jnp.bfloat16)
    d_up = (d_hidden * activated).astype(jnp.bfloat16)
    partial = jnp.concatenate(
        [outer_rows(arrived, d_gate), outer_rows(arrived, d_up), outer_rows(arrived_cot, hidden)],
        axis=1,
    ).astype(jnp.bfloat16)
    summed = lax.psum_scatter(partial, "expert", scatter_dimension=0, tiled=True)
    produced = rows_t(hidden, down_mat).astype(jnp.bfloat16)
    d_pick = (rows_t(d_gate, gate_mat) + rows_t(d_up, up_mat)).astype(jnp.bfloat16)
    back_out = exchange(produced)
    back_grad = exchange(d_pick)
    layer_output = (
        gains[0][:, None] * outer_rows(first, back_out)
        + gains[1][:, None] * outer_rows(second, back_out)
    ).astype(jnp.bfloat16)
    input_grad = (outer_rows(first, back_grad) + outer_rows(second, back_grad)).astype(jnp.bfloat16)
    summed = lax.ppermute(summed, ("dp", "expert"), flip)
    grad_gate = summed[None, :, :hidden_units]
    grad_up = summed[None, :, hidden_units : 2 * hidden_units]
    grad_down = summed[None, :, 2 * hidden_units :]
    return (layer_output, input_grad, grad_gate, grad_up, grad_down)


def solution(mesh):
    rows = P(("dp", "expert"), None)
    weights = P("expert", None, None)
    shares = P("expert", "dp", None)
    return jax.shard_map(
        shards,
        mesh=mesh,
        in_specs=(rows, rows, rows, rows, weights, weights, weights),
        out_specs=(rows, rows, shares, shares, shares),
        check_vma=False,
    )
```

profile of v0, /device:TPU:14, one launch (start us, length us, event | category | flops | bytes accessed | tf_op | source)
XLA Modules:
  0.0 330.9 jit_solution(815282746643636325)
XLA Ops:
  7.3 1.8 copy-done
  10.3 7.4 %collective-permute-start = (bf16[128,2304]{1,0:T(8,128)(2,1)S(1)}, bf16[128,2304]{1,0:T(8,128)(2,1)S(1)}, u32[]{:S(2)}, u32[]{:S(2)}) collective-permute-start(bf16[128,2304]{1,0:T(8,128)(2,1)S(1)} %pad_maximum_fusion.1), channel_id=1, source_target_pairs={{0,0},{1,16},{2,32},{3,48},{4,64},{5,80},{6,96},{7,112},{8,128},{9... | collective-permute-start | bytes 1769480 | tf_op jit(solution)/shard_map/ppermute | solution.py:55
  17.7 56.6 %collective-permute-done = bf16[128,2304]{1,0:T(8,128)(2,1)S(1)} collective-permute-done((bf16[128,2304]{1,0:T(8,128)(2,1)S(1)}, bf16[128,2304]{1,0:T(8,128)(2,1)S(1)}, u32[]{:S(2)}, u32[]{:S(2)}) %collective-permute-start) | collective-permute-done | bytes 589856 | tf_op jit(solution)/shard_map/ppermute | solution.py:55
  76.0 2.1 multiply_convert_fusion
  78.1 5.6 %all-to-all-start.2 = ((bf16[16,32,2048]{2,1,0:T(8,128)(2,1)}), bf16[16,32,2048]{2,1,0:T(8,128)(2,1)S(1)}, u32[]{:S(2)}, u32[]{:S(2)}) async-start(bf16[16,32,2048]{2,1,0:T(8,128)(2,1)} %bitcast.72), calls=%async_computation.2 | async-start | bytes 4194304 | tf_op jit(solution)/shard_map/all_to_all | solution.py:73
  83.7 2.1 convolution_convert_fusion.3
  85.8 23.9 %all-to-all-done.2 = bf16[16,32,2048]{2,1,0:T(8,128)(2,1)S(1)} async-done(((bf16[16,32,2048]{2,1,0:T(8,128)(2,1)}), bf16[16,32,2048]{2,1,0:T(8,128)(2,1)S(1)}, u32[]{:S(2)}, u32[]{:S(2)}) %all-to-all-start.2) | async-done | bytes 2097184 | tf_op jit(solution)/shard_map/all_to_all | solution.py:73
  109.6 7.3 %all-to-all-start = ((bf16[16,32,2048]{2,1,0:T(8,128)(2,1)}), bf16[16,32,2048]{2,1,0:T(8,128)(2,1)}, u32[]{:S(2)}, u32[]{:S(2)}) async-start(bf16[16,32,2048]{2,1,0:T(8,128)(2,1)} %bitcast.5), calls=%async_computation | async-start | bytes 4194304 | tf_op jit(solution)/shard_map/all_to_all | solution.py:73
  117.2 18.1 %all-gather.2.cloned.1.call-done = bf16[2048,2304]{1,0:T(8,128)(2,1)} async-done(((bf16[128,2304]{1,0:T(8,128)(2,1)}), bf16[2048,2304]{1,0:T(8,128)(2,1)}) %all-gather.2.cloned.1.call-update) | async-done | bytes 9437200 | tf_op jit(solution)/shard_map/all_gather | solution.py:56
  135.3 4.8 %fusion = f32[512,768]{1,0:T(8,128)} fusion(bf16[512,2048]{1,0:T(8,128)(2,1)S(1)} %bitcast.68, bf16[2048,2304]{1,0:T(8,128)(2,1)} %all-gather.2.cloned.1.call-done), kind=kOutput, calls=%fused_computation.8 | convolution fusion | flops 1610612736 | bytes 6815744 | tf_op jit(solution)/shard_map/dot_general | solution.py:83
  140.2 4.4 %fusion.5 = f32[512,768]{1,0:T(8,128)S(1)} fusion(bf16[512,2048]{1,0:T(8,128)(2,1)} %bitcast.6, bf16[2048,2304]{1,0:T(8,128)(2,1)} %all-gather.2.cloned.1.call-done), kind=kOutput, calls=%fused_computation.13 | convolution fusion | flops 1610612736 | bytes 6815744 | tf_op jit(solution)/shard_map/dot_general | solution.py:79
  144.7 5.0 %multiply_convert_fusion.2 = (bf16[512,768]{1,0:T(8,128)(2,1)S(1)}, bf16[512,768]{1,0:T(8,128)(2,1)S(1)}, bf16[512,768]{1,0:T(8,128)(2,1)S(1)}) fusion(f32[512,768]{1,0:T(8,128)S(1)} %copy-done.16, f32[512,768]{1,0:T(8,128)S(1)} %fusion.5, bf16[512,2048]{1,0:T(8,128)(2,1)} %bitcast.6, bf16[2048,2304]{1,0:T(8,128)(2,1)} %all-gather.2.cloned.1.call-done), kind=kOutput, calls=%fused_computation.25 | convolution fusion | flops 1616510976 | bytes 10747904 | tf_op jit(solution)/shard_map/dot_general | solution.py:78
  149.7 1.8 convolution_convert_fusion
  151.6 3.4 %convolution_convert_fusion.1 = bf16[2048,768]{0,1:T(8,128)(2,1)S(1)} fusion(bf16[512,2048]{1,0:T(8,128)(2,1)} %bitcast.6, bf16[512,768]{1,0:T(8,128)(2,1)S(1)} %get-tuple-element.26), kind=kOutput, calls=%fused_computation.4 | convolution fusion | flops 1612185600 | bytes 6029312 | tf_op jit(solution)/shard_map/dot_general | solution.py:36
  155.0 3.4 %convolution_convert_fusion.2 = bf16[2048,768]{0,1:T(8,128)(2,1)S(1)} fusion(bf16[512,2048]{1,0:T(8,128)(2,1)} %bitcast.6, bf16[512,768]{1,0:T(8,128)(2,1)S(1)} %get-tuple-element.25), kind=kOutput, calls=%fused_computation.5 | convolution fusion | flops 1612185600 | bytes 6029312 | tf_op jit(solution)/shard_map/dot_general | solution.py:36
  158.5 4.7 %pad_maximum_fusion = bf16[2048,2304]{0,1:T(8,128)(2,1)} fusion(bf16[2048,768]{0,1:T(8,128)(2,1)S(1)} %convolution_convert_fusion, bf16[2048,768]{0,1:T(8,128)(2,1)S(1)} %convolution_convert_fusion.1, bf16[2048,768]{0,1:T(8,128)(2,1)S(1)} %convolution_convert_fusion.2), kind=kLoop, calls=%fused_computation | loop fusion | flops 28311552 | bytes 18874368 | tf_op jit(solution)/shard_map/concatenate | solution.py:86
  163.1 12.4 %copy.25 = bf16[2048,2304]{1,0:T(8,128)(2,1)} copy(bf16[2048,2304]{0,1:T(8,128)(2,1)} %pad_maximum_fusion) | data formatting | bytes 18874368
  176.6 3.8 %fusion.3 = f32[512,2048]{1,0:T(8,128)S(1)} fusion(bf16[512,768]{1,0:T(8,128)(2,1)S(1)} %copy-done.15, bf16[2048,2304]{1,0:T(8,128)(2,1)} %all-gather.2.cloned.1.call-done), kind=kOutput, calls=%fused_computation.11 | convolution fusion | flops 1610612736 | bytes 8126464 | tf_op jit(solution)/shard_map/dot_general | solution.py:30
  180.4 5.1 %add_convert_fusion = bf16[512,2048]{1,0:T(8,128)(2,1)} fusion(f32[512,2048]{1,0:T(8,128)S(1)} %fusion.3, bf16[512,768]{1,0:T(8,128)(2,1)S(1)} %copy-done.13, bf16[2048,2304]{1,0:T(8,128)(2,1)} %all-gather.2.cloned.1.call-done), kind=kOutput, calls=%fused_computation.1 | convolution fusion | flops 1612709888 | bytes 10223616 | tf_op jit(solution)/shard_map/dot_general | solution.py:30
  185.5 8.2 %all-to-all-start.3 = ((bf16[16,32,2048]{2,1,0:T(8,128)(2,1)}), bf16[16,32,2048]{2,1,0:T(8,128)(2,1)S(1)}, u32[]{:S(2)}, u32[]{:S(2)}) async-start(bf16[16,32,2048]{2,1,0:T(8,128)(2,1)} %bitcast.71), calls=%async_computation.3 | async-start | bytes 4194304 | tf_op jit(solution)/shard_map/all_to_all | solution.py:73
  193.8 5.0 %convolution_convert_fusion.4 = bf16[512,2048]{1,0:T(8,128)(2,1)} fusion(bf16[512,768]{1,0:T(8,128)(2,1)S(1)} %copy-done.18, bf16[2048,2304]{1,0:T(8,128)(2,1)} %all-gather.2.cloned.1.call-done), kind=kOutput, calls=%fused_computation.7 | convolution fusion | flops 1611661312 | bytes 6029312 | tf_op jit(solution)/shard_map/dot_general | solution.py:30
  198.8 21.2 %all-to-all-done.3 = bf16[16,32,2048]{2,1,0:T(8,128)(2,1)S(1)} async-done(((bf16[16,32,2048]{2,1,0:T(8,128)(2,1)}), bf16[16,32,2048]{2,1,0:T(8,128)(2,1)S(1)}, u32[]{:S(2)}, u32[]{:S(2)}) %all-to-all-start.3) | async-done | bytes 2097184 | tf_op jit(solution)/shard_map/all_to_all | solution.py:73
  221.3 7.0 %all-to-all-start.1 = ((bf16[16,32,2048]{2,1,0:T(8,128)(2,1)}), bf16[16,32,2048]{2,1,0:T(8,128)(2,1)S(1)}, u32[]{:S(2)}, u32[]{:S(2)}) async-start(bf16[16,32,2048]{2,1,0:T(8,128)(2,1)} %bitcast.70), calls=%async_computation.1 | async-start | bytes 4194304 | tf_op jit(solution)/shard_map/all_to_all | solution.py:73
  228.4 2.3 fusion.15
  230.7 1.4 fusion.11
  232.1 20.1 %reduce-scatter.4.cloned.1.call-done = bf16[128,2304]{1,0:T(8,128)(2,1)} async-done(((bf16[2048,2304]{1,0:T(8,128)(2,1)}), bf16[128,2304]{1,0:T(8,128)(2,1)}) %reduce-scatter.4.cloned.1.call-update) | async-done | bytes 589840
  252.2 2.1 copy.26
  254.4 1.9 collective-permute-start.1
  258.2 3.2 fusion.12
  261.3 57.5 %collective-permute-done.1 = bf16[128,2304]{0,1:T(8,128)(2,1)} collective-permute-done((bf16[128,2304]{0,1:T(8,128)(2,1)}, bf16[128,2304]{0,1:T(8,128)(2,1)}, u32[]{:S(2)}, u32[]{:S(2)}) %collective-permute-start.1) | collective-permute-done | bytes 589856 | tf_op jit(solution)/shard_map/ppermute | solution.py:100
  318.8 1.8 slice_bitcast_fusion.2
  320.6 1.7 copy.22
  (59 shorter events, 9.2 us)
Async XLA Ops:
  7.2 1.9 copy-start
  7.2 68.0 %copy-start.10 = (f32[160,2]{0,1:T(2,128)S(1)}, f32[160,2]{0,1:T(2,128)}, u32[]{:S(2)}) copy-start(f32[160,2]{0,1:T(2,128)} %param.9) | copy-start | bytes 3844
  7.2 68.1 %copy-start.9 = (s32[160,2]{0,1:T(2,128)S(1)}, s32[160,2]{0,1:T(2,128)}, u32[]{:S(2)}) copy-start(s32[160,2]{0,1:T(2,128)} %param.8) | copy-start | bytes 3844
  7.2 128.1 %all-gather.2.cloned.1.call-start = ((), (), s32[]{:S(2)}) async-start(), calls=%async_computation.5 | async-start | bytes 10027008 | tf_op jit(solution)/shard_map/all_gather | solution.py:56
  9.1 66.9 %copy-start.11 = (bf16[160,2048]{1,0:T(8,128)(2,1)S(1)}, bf16[160,2048]{1,0:T(8,128)(2,1)}, u32[]{:S(2)}) copy-start(bf16[160,2048]{1,0:T(8,128)(2,1)} %param.10) | copy-start | bytes 1966084
  10.3 64.1 %collective-permute-start = (bf16[128,2304]{1,0:T(8,128)(2,1)S(1)}, bf16[128,2304]{1,0:T(8,128)(2,1)S(1)}, u32[]{:S(2)}, u32[]{:S(2)}) collective-permute-start(bf16[128,2304]{1,0:T(8,128)(2,1)S(1)} %pad_maximum_fusion.1), channel_id=1, source_target_pairs={{0,0},{1,16},{2,32},{3,48},{4,64},{5,80},{6,96},{7,112},{8,128},{9... | collective-permute-start | bytes 1769480 | tf_op jit(solution)/shard_map/ppermute | solution.py:55
  74.3 0.8 copy-start.8
  78.1 5.6 %copy-start.7 = (bf16[160,2048]{1,0:T(8,128)(2,1)S(1)}, bf16[160,2048]{1,0:T(8,128)(2,1)}, u32[]{:S(2)}) copy-start(bf16[160,2048]{1,0:T(8,128)(2,1)} %param.7) | copy-start | bytes 1966084
  78.1 31.5 %all-to-all-start.2 = ((bf16[16,32,2048]{2,1,0:T(8,128)(2,1)}), bf16[16,32,2048]{2,1,0:T(8,128)(2,1)S(1)}, u32[]{:S(2)}, u32[]{:S(2)}) async-start(bf16[16,32,2048]{2,1,0:T(8,128)(2,1)} %bitcast.72), calls=%async_computation.2 | async-start | bytes 4194304 | tf_op jit(solution)/shard_map/all_to_all | solution.py:73
  109.6 25.7 %copy-start.5 = (bf16[16,32,2048]{2,1,0:T(8,128)(2,1)}, bf16[16,32,2048]{2,1,0:T(8,128)(2,1)S(1)}, u32[]{:S(2)}) copy-start(bf16[16,32,2048]{2,1,0:T(8,128)(2,1)S(1)} %all-to-all-done.2) | copy-start | bytes 6291460
  109.6 30.6 %all-to-all-start = ((bf16[16,32,2048]{2,1,0:T(8,128)(2,1)}), bf16[16,32,2048]{2,1,0:T(8,128)(2,1)}, u32[]{:S(2)}, u32[]{:S(2)}) async-start(bf16[16,32,2048]{2,1,0:T(8,128)(2,1)} %bitcast.5), calls=%async_computation | async-start | bytes 4194304 | tf_op jit(solution)/shard_map/all_to_all | solution.py:73
  117.0 135.2 %reduce-scatter.4.cloned.1.call-start = ((), (), s32[]{:S(2)}) async-start(), calls=%async_computation.6 | async-start | bytes 10027008
  140.2 4.4 %copy-start.16 = (f32[512,768]{1,0:T(8,128)S(1)}, f32[512,768]{1,0:T(8,128)}, u32[]{:S(2)}) copy-start(f32[512,768]{1,0:T(8,128)} %fusion) | copy-start | bytes 4718596
  144.7 5.0 %copy-start.6 = (bf16[16,32,2048]{2,1,0:T(8,128)(2,1)S(1)}, bf16[16,32,2048]{2,1,0:T(8,128)(2,1)}, u32[]{:S(2)}) copy-start(bf16[16,32,2048]{2,1,0:T(8,128)(2,1)} %copy-done.5) | copy-start | bytes 6291460
  149.7 1.9 copy-start.17
  149.7 1.9 copy-start.14
  149.7 5.3 %copy-start.12 = (bf16[512,768]{1,0:T(8,128)(2,1)}, bf16[512,768]{1,0:T(8,128)(2,1)S(1)}, u32[]{:S(2)}) copy-start(bf16[512,768]{1,0:T(8,128)(2,1)S(1)} %get-tuple-element.25) | copy-start | bytes 2359300
  175.5 1.1 copy-start.15
  176.6 3.8 %copy-start.13 = (bf16[512,768]{1,0:T(8,128)(2,1)S(1)}, bf16[512,768]{1,0:T(8,128)(2,1)}, u32[]{:S(2)}) copy-start(bf16[512,768]{1,0:T(8,128)(2,1)} %copy-done.12) | copy-start | bytes 2359300
  185.5 8.3 %copy-start.18 = (bf16[512,768]{1,0:T(8,128)(2,1)S(1)}, bf16[512,768]{1,0:T(8,128)(2,1)}, u32[]{:S(2)}) copy-start(bf16[512,768]{1,0:T(8,128)(2,1)} %copy-done.17) | copy-start | bytes 2359300
  185.5 34.5 %all-to-all-start.3 = ((bf16[16,32,2048]{2,1,0:T(8,128)(2,1)}), bf16[16,32,2048]{2,1,0:T(8,128)(2,1)S(1)}, u32[]{:S(2)}, u32[]{:S(2)}) async-start(bf16[16,32,2048]{2,1,0:T(8,128)(2,1)} %bitcast.71), calls=%async_computation.3 | async-start | bytes 4194304 | tf_op jit(solution)/shard_map/all_to_all | solution.py:73
  220.0 1.4 copy-start.3
  221.3 34.9 %all-to-all-start.1 = ((bf16[16,32,2048]{2,1,0:T(8,128)(2,1)}), bf16[16,32,2048]{2,1,0:T(8,128)(2,1)S(1)}, u32[]{:S(2)}, u32[]{:S(2)}) async-start(bf16[16,32,2048]{2,1,0:T(8,128)(2,1)} %bitcast.70), calls=%async_computation.1 | async-start | bytes 4194304 | tf_op jit(solution)/shard_map/all_to_all | solution.py:73
  228.4 2.4 copy-start.4
  254.4 64.5 %collective-permute-start.1 = (bf16[128,2304]{0,1:T(8,128)(2,1)}, bf16[128,2304]{0,1:T(8,128)(2,1)}, u32[]{:S(2)}, u32[]{:S(2)}) collective-permute-start(bf16[128,2304]{0,1:T(8,128)(2,1)} %copy.26), channel_id=1, source_target_pairs={{0,0},{1,16},{2,32},{3,48},{4,64},{5,80},{6,96},{7,112},{8,128},{9... | collective-permute-start | bytes 1769480 | tf_op jit(solution)/shard_map/ppermute | solution.py:100
  256.3 1.4 copy-start.2
  258.2 65.9 %copy-start.1 = (bf16[1,2048,768]{2,1,0:T(8,128)(2,1)S(1)}, bf16[1,2048,768]{2,1,0:T(8,128)(2,1)}, u32[]{:S(2)}) copy-start(bf16[1,2048,768]{2,1,0:T(8,128)(2,1)} %param.11) | copy-start | bytes 9437188
Sparse Core Ops, SparseCore 0:
  75.3 59.9 all-gather.1
  175.6 76.5 reduce-scatter.3
where the time goes:
time: 332 us; the launch traced here: 331 us
  waiting for transfers between devices  198 us (60%)
  matrix products  48.6 us (15%)
  starting transfers between devices  37.8 us (11%)
  local copies, waits for them, and re-layouts  27.6 us (8%)
  between operations  14.3 us (4%)
  other arithmetic  5.04 us (2%)
    ppermute x1, waiting for transfers between devices, shards(): summed = lax.ppermute(summed, ('dp', 'expert'), flip)  57.5 us
    ppermute x1, waiting for transfers between devices, shards(): part = lax.ppermute(part, ('dp', 'expert'), flip)  56.6 us
    all_to_all x4, waiting for transfers between devices, exchange(): block = lax.all_to_all(block, 'dp', split_axis=0, concat_axis=0, tiled=True)  45.1 us
    all_to_all x4, starting transfers between devices, exchange(): block = lax.all_to_all(block, 'dp', split_axis=0, concat_axis=0, tiled=True)  28.2 us
    unnamed x43, local copies, waits for them, and re-layouts  24.4 us
    unnamed x3, waiting for transfers between devices  20.2 us
    all_gather x1, waiting for transfers between devices, shards(): full = lax.all_gather(part, 'expert', axis=0, tiled=True)  18.1 us
    dot_general x7, matrix products, outer_rows(): lax.dot_general(left, right, (((0,), (0,)), ((), ())), preferred_element_...  16.1 us
  transfers between devices with their start and end apart: 8, of which 7 were waited for; matrix products, arithmetic and copies ran while one was open for 10% of the time, Pallas kernels for 0%

commit v1 on v0

--- a/solution.py
+++ b/solution.py
@@ -53,7 +53,14 @@
 
     part = jnp.concatenate([fetch(w_gate), fetch(w_up), fetch(w_down)], axis=1)
     part = lax.ppermute(part, ("dp", "expert"), flip)
-    full = lax.all_gather(part, "expert", axis=0, tiled=True)
+    ring = [part]
+    for hop in range(15):
+        ring.append(lax.ppermute(ring[-1], "expert", [(dev, (dev + 1) % 16) for dev in range(16)]))
+    full = jnp.roll(
+        jnp.concatenate(ring[::-1], axis=0),
+        (lax.axis_index("expert") + 1) * ring[0].shape[0],
+        axis=0,
+    )
     gate_mat = full[:, :hidden_units]
     up_mat = full[:, hidden_units : 2 * hidden_units]
     down_mat = full[:, 2 * hidden_units :]

time: 332 us -> 499 us (1.50)
  waiting for transfers between devices: 198 us -> 311 us
  local copies, waits for them, and re-layouts: 27.6 us -> 69.3 us
  matrix products: 48.6 us -> 54.6 us
    ppermute x0 -> x15, waiting for transfers between devices: none -> 143 us  [shards(): lax.ppermute(ring[-1], 'expert', [(dev, (dev + 1) % 16) for dev in range(...]
    unnamed x43 -> x84, local copies, waits for them, and re-layouts: 24.4 us -> 64.6 us
    all_to_all x4, waiting for transfers between devices: 45.1 us -> 22.6 us  [exchange(): block = lax.all_to_all(block, 'dp', split_axis=0, concat_axis=0, tiled=True)]
    all_gather x1 -> x0, waiting for transfers between devices: 18.1 us -> none  [shards(): full = lax.all_gather(part, 'expert', axis=0, tiled=True)]
    unnamed x3 -> x2, waiting for transfers between devices: 20.2 us -> 30.9 us
  transfers between devices with their start and end apart: 8 -> 22, of which waited for: 7 -> 19; matrix products, arithmetic and copies ran while one was open for 10% -> 15% of each run, Pallas kernels for 0% -> 0%
where the time goes in v1:
time: 499 us; the launch traced here: 497 us
  waiting for transfers between devices  311 us (62%)
  local copies, waits for them, and re-layouts  69.3 us (14%)
  matrix products  54.6 us (11%)
  starting transfers between devices  42 us (8%)
  between operations  14.3 us (3%)
  other arithmetic  5.83 us (1%)
    ppermute x15, waiting for transfers between devices, shards(): lax.ppermute(ring[-1], 'expert', [(dev, (dev + 1) % 16) for dev in range(...  143 us
    unnamed x84, local copies, waits for them, and re-layouts  64.6 us
    ppermute x1, waiting for transfers between devices, shards(): summed = lax.ppermute(summed, ('dp', 'expert'), flip)  57.5 us
    ppermute x1, waiting for transfers between devices, shards(): part = lax.ppermute(part, ('dp', 'expert'), flip)  56.6 us
    all_to_all x4, starting transfers between devices, exchange(): block = lax.all_to_all(block, 'dp', split_axis=0, concat_axis=0, tiled=True)  32.4 us
    unnamed x2, waiting for transfers between devices  30.9 us
    all_to_all x4, waiting for transfers between devices, exchange(): block = lax.all_to_all(block, 'dp', split_axis=0, concat_axis=0, tiled=True)  22.6 us
    dot_general x7, matrix products, outer_rows(): lax.dot_general(left, right, (((0,), (0,)), ((), ())), preferred_element_...  19.9 us
  transfers between devices with their start and end apart: 22, of which 19 were waited for; matrix products, arithmetic and copies ran while one was open for 15% of the time, Pallas kernels for 0%

profile of v1, /device:TPU:14, one launch (start us, length us, event | category | flops | bytes accessed | tf_op | source)
XLA Modules:
  0.0 497.0 jit_solution(16677216725485037382)
XLA Ops:
  10.2 7.4 %collective-permute-start = (bf16[128,2304]{1,0:T(8,128)(2,1)S(1)}, bf16[128,2304]{1,0:T(8,128)(2,1)S(1)}, u32[]{:S(2)}, u32[]{:S(2)}) collective-permute-start(bf16[128,2304]{1,0:T(8,128)(2,1)S(1)} %pad_maximum_fusion.1), channel_id=1, source_target_pairs={{0,0},{1,16},{2,32},{3,48},{4,64},{5,80},{6,96},{7,112},{8,128},{9... | collective-permute-start | bytes 1769480 | tf_op jit(solution)/shard_map/ppermute | solution.py:55
  17.6 56.6 %collective-permute-done = bf16[128,2304]{1,0:T(8,128)(2,1)S(1)} collective-permute-done((bf16[128,2304]{1,0:T(8,128)(2,1)S(1)}, bf16[128,2304]{1,0:T(8,128)(2,1)S(1)}, u32[]{:S(2)}, u32[]{:S(2)}) %collective-permute-start) | collective-permute-done | bytes 589856 | tf_op jit(solution)/shard_map/ppermute | solution.py:55
  74.3 10.5 %collective-permute-done.1 = bf16[128,2304]{1,0:T(8,128)(2,1)S(1)} collective-permute-done((bf16[128,2304]{1,0:T(8,128)(2,1)S(1)}, bf16[128,2304]{1,0:T(8,128)(2,1)S(1)}, u32[]{:S(2)}, u32[]{:S(2)}) %collective-permute-start.1) | collective-permute-done | bytes 589856 | tf_op jit(solution)/shard_map/ppermute | solution.py:58
  84.8 10.5 %collective-permute-done.2 = bf16[128,2304]{1,0:T(8,128)(2,1)S(1)} collective-permute-done((bf16[128,2304]{1,0:T(8,128)(2,1)S(1)}, bf16[128,2304]{1,0:T(8,128)(2,1)S(1)}, u32[]{:S(2)}, u32[]{:S(2)}) %collective-permute-start.2) | collective-permute-done | bytes 589856 | tf_op jit(solution)/shard_map/ppermute | solution.py:58
  95.3 10.5 %collective-permute-done.3 = bf16[128,2304]{1,0:T(8,128)(2,1)S(1)} collective-permute-done((bf16[128,2304]{1,0:T(8,128)(2,1)S(1)}, bf16[128,2304]{1,0:T(8,128)(2,1)S(1)}, u32[]{:S(2)}, u32[]{:S(2)}) %collective-permute-start.3) | collective-permute-done | bytes 589856 | tf_op jit(solution)/shard_map/ppermute | solution.py:58
  105.8 10.5 %collective-permute-done.4 = bf16[128,2304]{1,0:T(8,128)(2,1)S(1)} collective-permute-done((bf16[128,2304]{1,0:T(8,128)(2,1)S(1)}, bf16[128,2304]{1,0:T(8,128)(2,1)S(1)}, u32[]{:S(2)}, u32[]{:S(2)}) %collective-permute-start.4) | collective-permute-done | bytes 589856 | tf_op jit(solution)/shard_map/ppermute | solution.py:58
  116.4 10.5 %collective-permute-done.5 = bf16[128,2304]{1,0:T(8,128)(2,1)S(1)} collective-permute-done((bf16[128,2304]{1,0:T(8,128)(2,1)S(1)}, bf16[128,2304]{1,0:T(8,128)(2,1)S(1)}, u32[]{:S(2)}, u32[]{:S(2)}) %collective-permute-start.5) | collective-permute-done | bytes 589856 | tf_op jit(solution)/shard_map/ppermute | solution.py:58
  127.7 10.5 %collective-permute-done.6 = bf16[128,2304]{1,0:T(8,128)(2,1)S(1)} collective-permute-done((bf16[128,2304]{1,0:T(8,128)(2,1)S(1)}, bf16[128,2304]{1,0:T(8,128)(2,1)S(1)}, u32[]{:S(2)}, u32[]{:S(2)}) %collective-permute-start.6) | collective-permute-done | bytes 589856 | tf_op jit(solution)/shard_map/ppermute | solution.py:58
  139.1 10.5 %collective-permute-done.7 = bf16[128,2304]{1,0:T(8,128)(2,1)S(1)} collective-permute-done((bf16[128,2304]{1,0:T(8,128)(2,1)S(1)}, bf16[128,2304]{1,0:T(8,128)(2,1)S(1)}, u32[]{:S(2)}, u32[]{:S(2)}) %collective-permute-start.7) | collective-permute-done | bytes 589856 | tf_op jit(solution)/shard_map/ppermute | solution.py:58
  150.4 10.5 %collective-permute-done.8 = bf16[128,2304]{1,0:T(8,128)(2,1)S(1)} collective-permute-done((bf16[128,2304]{1,0:T(8,128)(2,1)S(1)}, bf16[128,2304]{1,0:T(8,128)(2,1)S(1)}, u32[]{:S(2)}, u32[]{:S(2)}) %collective-permute-start.8) | collective-permute-done | bytes 589856 | tf_op jit(solution)/shard_map/ppermute | solution.py:58
  161.8 10.5 %collective-permute-done.9 = bf16[128,2304]{1,0:T(8,128)(2,1)S(1)} collective-permute-done((bf16[128,2304]{1,0:T(8,128)(2,1)S(1)}, bf16[128,2304]{1,0:T(8,128)(2,1)S(1)}, u32[]{:S(2)}, u32[]{:S(2)}) %collective-permute-start.9) | collective-permute-done | bytes 589856 | tf_op jit(solution)/shard_map/ppermute | solution.py:58
  173.1 10.5 %collective-permute-done.10 = bf16[128,2304]{1,0:T(8,128)(2,1)S(1)} collective-permute-done((bf16[128,2304]{1,0:T(8,128)(2,1)S(1)}, bf16[128,2304]{1,0:T(8,128)(2,1)S(1)}, u32[]{:S(2)}, u32[]{:S(2)}) %collective-permute-start.10) | collective-permute-done | bytes 589856 | tf_op jit(solution)/shard_map/ppermute | solution.py:58
  184.4 10.5 %collective-permute-done.11 = bf16[128,2304]{1,0:T(8,128)(2,1)S(1)} collective-permute-done((bf16[128,2304]{1,0:T(8,128)(2,1)S(1)}, bf16[128,2304]{1,0:T(8,128)(2,1)S(1)}, u32[]{:S(2)}, u32[]{:S(2)}) %collective-permute-start.11) | collective-permute-done | bytes 589856 | tf_op jit(solution)/shard_map/ppermute | solution.py:58
  195.8 10.6 %collective-permute-done.12 = bf16[128,2304]{1,0:T(8,128)(2,1)} collective-permute-done((bf16[128,2304]{1,0:T(8,128)(2,1)S(1)}, bf16[128,2304]{1,0:T(8,128)(2,1)}, u32[]{:S(2)}, u32[]{:S(2)}) %collective-permute-start.12) | collective-permute-done | bytes 589856 | tf_op jit(solution)/shard_map/ppermute | solution.py:58
  207.4 9.8 %collective-permute-done.13 = bf16[128,2304]{1,0:T(8,128)(2,1)} collective-permute-done((bf16[128,2304]{1,0:T(8,128)(2,1)}, bf16[128,2304]{1,0:T(8,128)(2,1)}, u32[]{:S(2)}, u32[]{:S(2)}) %collective-permute-start.13) | collective-permute-done | bytes 589856 | tf_op jit(solution)/shard_map/ppermute | solution.py:58
  221.4 6.9 %all-to-all-start = ((bf16[16,32,2048]{2,1,0:T(8,128)(2,1)}), bf16[16,32,2048]{2,1,0:T(8,128)(2,1)}, u32[]{:S(2)}, u32[]{:S(2)}) async-start(bf16[16,32,2048]{2,1,0:T(8,128)(2,1)} %bitcast.5), calls=%async_computation | async-start | bytes 4194304 | tf_op jit(solution)/shard_map/all_to_all | solution.py:80
  231.9 7.2 %collective-permute-done.15 = bf16[128,2304]{1,0:T(8,128)(2,1)S(1)} collective-permute-done((bf16[128,2304]{1,0:T(8,128)(2,1)}, bf16[128,2304]{1,0:T(8,128)(2,1)S(1)}, u32[]{:S(2)}, u32[]{:S(2)}) %collective-permute-start.15) | collective-permute-done | bytes 589856 | tf_op jit(solution)/shard_map/ppermute | solution.py:58
  273.2 7.2 %all-to-all-start.2 = ((bf16[16,32,2048]{2,1,0:T(8,128)(2,1)}), bf16[16,32,2048]{2,1,0:T(8,128)(2,1)}, u32[]{:S(2)}, u32[]{:S(2)}) async-start(bf16[16,32,2048]{2,1,0:T(8,128)(2,1)} %bitcast.66), calls=%async_computation.2 | async-start | bytes 4194304 | tf_op jit(solution)/shard_map/all_to_all | solution.py:80
  284.9 4.3 fusion.8
  289.3 10.1 %all-to-all-done.2 = bf16[16,32,2048]{2,1,0:T(8,128)(2,1)} async-done(((bf16[16,32,2048]{2,1,0:T(8,128)(2,1)}), bf16[16,32,2048]{2,1,0:T(8,128)(2,1)}, u32[]{:S(2)}, u32[]{:S(2)}) %all-to-all-start.2) | async-done | bytes 2097184 | tf_op jit(solution)/shard_map/all_to_all | solution.py:80
  299.4 4.3 fusion.3
  303.7 4.8 multiply_convert_fusion.2
  308.5 4.3 convolution_convert_fusion
  319.7 4.8 pad_maximum_fusion
  324.5 12.8 %copy.25 = bf16[2048,2304]{1,0:T(8,128)(2,1)} copy(bf16[2048,2304]{0,1:T(8,128)(2,1)} %pad_maximum_fusion) | data formatting | bytes 18874368
  342.2 5.1 %add_convert_fusion = bf16[512,2048]{1,0:T(8,128)(2,1)} fusion(f32[512,2048]{1,0:T(8,128)S(1)} %fusion.6, bf16[512,768]{1,0:T(8,128)(2,1)S(1)} %copy-done.21, bf16[4096,2304]{1,0:T(8,128)(2,1)} %constant_dynamic-update-slice_fusion, s32[]{:T(128)S(6)} %select_n.30), kind=kOutput, calls=%fused_computation.1 | convolution fusion | flops 1612709888 | bytes 10223620 | tf_op jit(solution)/shard_map/dot_general | solution.py:30
  347.3 7.6 %all-to-all-start.3 = ((bf16[16,32,2048]{2,1,0:T(8,128)(2,1)}), bf16[16,32,2048]{2,1,0:T(8,128)(2,1)S(1)}, u32[]{:S(2)}, u32[]{:S(2)}) async-start(bf16[16,32,2048]{2,1,0:T(8,128)(2,1)} %bitcast.68), calls=%async_computation.3 | async-start | bytes 4194304 | tf_op jit(solution)/shard_map/all_to_all | solution.py:80
  354.9 5.5 %convolution_convert_fusion.4 = bf16[512,2048]{1,0:T(8,128)(2,1)} fusion(bf16[512,768]{1,0:T(8,128)(2,1)S(1)} %copy-done.23, bf16[4096,2304]{1,0:T(8,128)(2,1)} %constant_dynamic-update-slice_fusion, s32[]{:T(128)S(6)} %select_n.30, s32[]{:T(128)S(6)} %add.61), kind=kOutput, calls=%fused_computation.7 | convolution fusion | flops 1611661312 | bytes 6029320 | tf_op jit(solution)/shard_map/dot_general | solution.py:30
  360.4 12.5 %all-to-all-done.3 = bf16[16,32,2048]{2,1,0:T(8,128)(2,1)S(1)} async-done(((bf16[16,32,2048]{2,1,0:T(8,128)(2,1)}), bf16[16,32,2048]{2,1,0:T(8,128)(2,1)S(1)}, u32[]{:S(2)}, u32[]{:S(2)}) %all-to-all-start.3) | async-done | bytes 2097184 | tf_op jit(solution)/shard_map/all_to_all | solution.py:80
  372.9 10.7 %all-to-all-start.1 = ((bf16[16,32,2048]{2,1,0:T(8,128)(2,1)}), bf16[16,32,2048]{2,1,0:T(8,128)(2,1)}, u32[]{:S(2)}, u32[]{:S(2)}) async-start(bf16[16,32,2048]{2,1,0:T(8,128)(2,1)} %bitcast.67), calls=%async_computation.1 | async-start | bytes 4194304 | tf_op jit(solution)/shard_map/all_to_all | solution.py:80
  387.3 30.9 %reduce-scatter.4.cloned.1.call-done = bf16[128,2304]{1,0:T(8,128)(2,1)} async-done(((bf16[2048,2304]{1,0:T(8,128)(2,1)}), bf16[128,2304]{1,0:T(8,128)(2,1)}) %reduce-scatter.4.cloned.1.call-update) | async-done | bytes 589840
  427.4 57.5 %collective-permute-done.16 = bf16[128,2304]{0,1:T(8,128)(2,1)} collective-permute-done((bf16[128,2304]{0,1:T(8,128)(2,1)}, bf16[128,2304]{0,1:T(8,128)(2,1)}, u32[]{:S(2)}, u32[]{:S(2)}) %collective-permute-start.16) | collective-permute-done | bytes 589856 | tf_op jit(solution)/shard_map/ppermute | solution.py:107
  (128 shorter events, 86.0 us)
Async XLA Ops:
  7.2 221.1 %copy-start.19 = (f32[160,2]{0,1:T(2,128)S(1)}, f32[160,2]{0,1:T(2,128)}, u32[]{:S(2)}) copy-start(f32[160,2]{0,1:T(2,128)} %param.9) | copy-start | bytes 3844
  10.2 64.1 %collective-permute-start = (bf16[128,2304]{1,0:T(8,128)(2,1)S(1)}, bf16[128,2304]{1,0:T(8,128)(2,1)S(1)}, u32[]{:S(2)}, u32[]{:S(2)}) collective-permute-start(bf16[128,2304]{1,0:T(8,128)(2,1)S(1)} %pad_maximum_fusion.1), channel_id=1, source_target_pairs={{0,0},{1,16},{2,32},{3,48},{4,64},{5,80},{6,96},{7,112},{8,128},{9... | collective-permute-start | bytes 1769480 | tf_op jit(solution)/shard_map/ppermute | solution.py:55
  74.3 10.5 %collective-permute-start.1 = (bf16[128,2304]{1,0:T(8,128)(2,1)S(1)}, bf16[128,2304]{1,0:T(8,128)(2,1)S(1)}, u32[]{:S(2)}, u32[]{:S(2)}) collective-permute-start(bf16[128,2304]{1,0:T(8,128)(2,1)S(1)} %collective-permute-done), channel_id=1, source_target_pairs={{0,1},{1,2},{2,3},{3,4},{4,5},{5,6},{6,7},{7,8},{8,9},{9,10},{10,1... | collective-permute-start | bytes 1769480 | tf_op jit(solution)/shard_map/ppermute | solution.py:58
  84.8 10.5 %collective-permute-start.2 = (bf16[128,2304]{1,0:T(8,128)(2,1)S(1)}, bf16[128,2304]{1,0:T(8,128)(2,1)S(1)}, u32[]{:S(2)}, u32[]{:S(2)}) collective-permute-start(bf16[128,2304]{1,0:T(8,128)(2,1)S(1)} %collective-permute-done.1), channel_id=1, source_target_pairs={{0,1},{1,2},{2,3},{3,4},{4,5},{5,6},{6,7},{7,8},{8,9},{9,10},{10,1... | collective-permute-start | bytes 1769480 | tf_op jit(solution)/shard_map/ppermute | solution.py:58
  95.3 10.5 %collective-permute-start.3 = (bf16[128,2304]{1,0:T(8,128)(2,1)S(1)}, bf16[128,2304]{1,0:T(8,128)(2,1)S(1)}, u32[]{:S(2)}, u32[]{:S(2)}) collective-permute-start(bf16[128,2304]{1,0:T(8,128)(2,1)S(1)} %collective-permute-done.2), channel_id=1, source_target_pairs={{0,1},{1,2},{2,3},{3,4},{4,5},{5,6},{6,7},{7,8},{8,9},{9,10},{10,1... | collective-permute-start | bytes 1769480 | tf_op jit(solution)/shard_map/ppermute | solution.py:58
  105.8 10.5 %collective-permute-start.4 = (bf16[128,2304]{1,0:T(8,128)(2,1)S(1)}, bf16[128,2304]{1,0:T(8,128)(2,1)S(1)}, u32[]{:S(2)}, u32[]{:S(2)}) collective-permute-start(bf16[128,2304]{1,0:T(8,128)(2,1)S(1)} %collective-permute-done.3), channel_id=1, source_target_pairs={{0,1},{1,2},{2,3},{3,4},{4,5},{5,6},{6,7},{7,8},{8,9},{9,10},{10,1... | collective-permute-start | bytes 1769480 | tf_op jit(solution)/shard_map/ppermute | solution.py:58
  116.4 10.5 %collective-permute-start.5 = (bf16[128,2304]{1,0:T(8,128)(2,1)S(1)}, bf16[128,2304]{1,0:T(8,128)(2,1)S(1)}, u32[]{:S(2)}, u32[]{:S(2)}) collective-permute-start(bf16[128,2304]{1,0:T(8,128)(2,1)S(1)} %collective-permute-done.4), channel_id=1, source_target_pairs={{0,1},{1,2},{2,3},{3,4},{4,5},{5,6},{6,7},{7,8},{8,9},{9,10},{10,1... | collective-permute-start | bytes 1769480 | tf_op jit(solution)/shard_map/ppermute | solution.py:58
  127.7 10.5 %collective-permute-start.6 = (bf16[128,2304]{1,0:T(8,128)(2,1)S(1)}, bf16[128,2304]{1,0:T(8,128)(2,1)S(1)}, u32[]{:S(2)}, u32[]{:S(2)}) collective-permute-start(bf16[128,2304]{1,0:T(8,128)(2,1)S(1)} %collective-permute-done.5), channel_id=1, source_target_pairs={{0,1},{1,2},{2,3},{3,4},{4,5},{5,6},{6,7},{7,8},{8,9},{9,10},{10,1... | collective-permute-start | bytes 1769480 | tf_op jit(solution)/shard_map/ppermute | solution.py:58
  139.1 10.5 %collective-permute-start.7 = (bf16[128,2304]{1,0:T(8,128)(2,1)S(1)}, bf16[128,2304]{1,0:T(8,128)(2,1)S(1)}, u32[]{:S(2)}, u32[]{:S(2)}) collective-permute-start(bf16[128,2304]{1,0:T(8,128)(2,1)S(1)} %collective-permute-done.6), channel_id=1, source_target_pairs={{0,1},{1,2},{2,3},{3,4},{4,5},{5,6},{6,7},{7,8},{8,9},{9,10},{10,1... | collective-permute-start | bytes 1769480 | tf_op jit(solution)/shard_map/ppermute | solution.py:58
  150.4 10.5 %collective-permute-start.8 = (bf16[128,2304]{1,0:T(8,128)(2,1)S(1)}, bf16[128,2304]{1,0:T(8,128)(2,1)S(1)}, u32[]{:S(2)}, u32[]{:S(2)}) collective-permute-start(bf16[128,2304]{1,0:T(8,128)(2,1)S(1)} %collective-permute-done.7), channel_id=1, source_target_pairs={{0,1},{1,2},{2,3},{3,4},{4,5},{5,6},{6,7},{7,8},{8,9},{9,10},{10,1... | collective-permute-start | bytes 1769480 | tf_op jit(solution)/shard_map/ppermute | solution.py:58
  161.8 10.5 %collective-permute-start.9 = (bf16[128,2304]{1,0:T(8,128)(2,1)S(1)}, bf16[128,2304]{1,0:T(8,128)(2,1)S(1)}, u32[]{:S(2)}, u32[]{:S(2)}) collective-permute-start(bf16[128,2304]{1,0:T(8,128)(2,1)S(1)} %collective-permute-done.8), channel_id=1, source_target_pairs={{0,1},{1,2},{2,3},{3,4},{4,5},{5,6},{6,7},{7,8},{8,9},{9,10},{10,1... | collective-permute-start | bytes 1769480 | tf_op jit(solution)/shard_map/ppermute | solution.py:58
  173.1 10.5 %collective-permute-start.10 = (bf16[128,2304]{1,0:T(8,128)(2,1)S(1)}, bf16[128,2304]{1,0:T(8,128)(2,1)S(1)}, u32[]{:S(2)}, u32[]{:S(2)}) collective-permute-start(bf16[128,2304]{1,0:T(8,128)(2,1)S(1)} %collective-permute-done.9), channel_id=1, source_target_pairs={{0,1},{1,2},{2,3},{3,4},{4,5},{5,6},{6,7},{7,8},{8,9},{9,10},{10,1... | collective-permute-start | bytes 1769480 | tf_op jit(solution)/shard_map/ppermute | solution.py:58
  184.4 10.5 %collective-permute-start.11 = (bf16[128,2304]{1,0:T(8,128)(2,1)S(1)}, bf16[128,2304]{1,0:T(8,128)(2,1)S(1)}, u32[]{:S(2)}, u32[]{:S(2)}) collective-permute-start(bf16[128,2304]{1,0:T(8,128)(2,1)S(1)} %collective-permute-done.10), channel_id=1, source_target_pairs={{0,1},{1,2},{2,3},{3,4},{4,5},{5,6},{6,7},{7,8},{8,9},{9,10},{10,1... | collective-permute-start | bytes 1769480 | tf_op jit(solution)/shard_map/ppermute | solution.py:58
  195.8 10.6 %collective-permute-start.12 = (bf16[128,2304]{1,0:T(8,128)(2,1)S(1)}, bf16[128,2304]{1,0:T(8,128)(2,1)}, u32[]{:S(2)}, u32[]{:S(2)}) collective-permute-start(bf16[128,2304]{1,0:T(8,128)(2,1)S(1)} %collective-permute-done.11), channel_id=1, source_target_pairs={{0,1},{1,2},{2,3},{3,4},{4,5},{5,6},{6,7},{7,8},{8,9},{9,10},{10,1... | collective-permute-start | bytes 1769480 | tf_op jit(solution)/shard_map/ppermute | solution.py:58
  206.4 10.8 %collective-permute-start.13 = (bf16[128,2304]{1,0:T(8,128)(2,1)}, bf16[128,2304]{1,0:T(8,128)(2,1)}, u32[]{:S(2)}, u32[]{:S(2)}) collective-permute-start(bf16[128,2304]{1,0:T(8,128)(2,1)} %collective-permute-done.12), channel_id=1, source_target_pairs={{0,1},{1,2},{2,3},{3,4},{4,5},{5,6},{6,7},{7,8},{8,9},{9,10},{10,1... | collective-permute-start | bytes 1769480 | tf_op jit(solution)/shard_map/ppermute | solution.py:58
  217.2 11.1 %collective-permute-start.14 = (bf16[128,2304]{1,0:T(8,128)(2,1)}, bf16[128,2304]{1,0:T(8,128)(2,1)}, u32[]{:S(2)}, u32[]{:S(2)}) collective-permute-start(bf16[128,2304]{1,0:T(8,128)(2,1)} %collective-permute-done.13), channel_id=1, source_target_pairs={{0,1},{1,2},{2,3},{3,4},{4,5},{5,6},{6,7},{7,8},{8,9},{9,10},{10,1... | collective-permute-start | bytes 1769480 | tf_op jit(solution)/shard_map/ppermute | solution.py:58
  221.4 51.8 %all-to-all-start = ((bf16[16,32,2048]{2,1,0:T(8,128)(2,1)}), bf16[16,32,2048]{2,1,0:T(8,128)(2,1)}, u32[]{:S(2)}, u32[]{:S(2)}) async-start(bf16[16,32,2048]{2,1,0:T(8,128)(2,1)} %bitcast.5), calls=%async_computation | async-start | bytes 4194304 | tf_op jit(solution)/shard_map/all_to_all | solution.py:80
  228.3 10.7 %collective-permute-start.15 = (bf16[128,2304]{1,0:T(8,128)(2,1)}, bf16[128,2304]{1,0:T(8,128)(2,1)S(1)}, u32[]{:S(2)}, u32[]{:S(2)}) collective-permute-start(bf16[128,2304]{1,0:T(8,128)(2,1)} %collective-permute-done.14), channel_id=1, source_target_pairs={{0,1},{1,2},{2,3},{3,4},{4,5},{5,6},{6,7},{7,8},{8,9},{9,10},{10,1... | collective-permute-start | bytes 1769480 | tf_op jit(solution)/shard_map/ppermute | solution.py:58
  228.5 24.9 %copy-start.8 = (bf16[128,2304]{1,0:T(8,128)(2,1)S(1)}, bf16[128,2304]{1,0:T(8,128)(2,1)}, u32[]{:S(2)}) copy-start(bf16[128,2304]{1,0:T(8,128)(2,1)} %copy-done.7) | copy-start | bytes 1769476
  228.5 25.8 %copy-start.6 = (bf16[128,2304]{1,0:T(8,128)(2,1)S(1)}, bf16[128,2304]{1,0:T(8,128)(2,1)}, u32[]{:S(2)}) copy-start(bf16[128,2304]{1,0:T(8,128)(2,1)} %copy-done.5) | copy-start | bytes 1769476
  231.9 23.3 %copy-start.4 = (bf16[128,2304]{1,0:T(8,128)(2,1)S(1)}, bf16[128,2304]{1,0:T(8,128)(2,1)}, u32[]{:S(2)}) copy-start(bf16[128,2304]{1,0:T(8,128)(2,1)} %copy-done.3) | copy-start | bytes 1769476
  254.3 12.8 %copy-start.16 = (bf16[128,2304]{1,0:T(8,128)(2,1)S(1)}, bf16[128,2304]{1,0:T(8,128)(2,1)}, u32[]{:S(2)}) copy-start(bf16[128,2304]{1,0:T(8,128)(2,1)} %copy-done.15) | copy-start | bytes 1769476
  255.2 12.8 %copy-start.14 = (bf16[128,2304]{1,0:T(8,128)(2,1)S(1)}, bf16[128,2304]{1,0:T(8,128)(2,1)}, u32[]{:S(2)}) copy-start(bf16[128,2304]{1,0:T(8,128)(2,1)} %copy-done.13) | copy-start | bytes 1769476
  256.0 12.8 %copy-start.12 = (bf16[128,2304]{1,0:T(8,128)(2,1)S(1)}, bf16[128,2304]{1,0:T(8,128)(2,1)}, u32[]{:S(2)}) copy-start(bf16[128,2304]{1,0:T(8,128)(2,1)} %copy-done.11) | copy-start | bytes 1769476
  256.9 12.9 %copy-start.10 = (bf16[128,2304]{1,0:T(8,128)(2,1)S(1)}, bf16[128,2304]{1,0:T(8,128)(2,1)}, u32[]{:S(2)}) copy-start(bf16[128,2304]{1,0:T(8,128)(2,1)} %copy-done.9) | copy-start | bytes 1769476
  273.2 26.2 %all-to-all-start.2 = ((bf16[16,32,2048]{2,1,0:T(8,128)(2,1)}), bf16[16,32,2048]{2,1,0:T(8,128)(2,1)}, u32[]{:S(2)}, u32[]{:S(2)}) async-start(bf16[16,32,2048]{2,1,0:T(8,128)(2,1)} %bitcast.66), calls=%async_computation.2 | async-start | bytes 4194304 | tf_op jit(solution)/shard_map/all_to_all | solution.py:80
  280.4 137.8 %reduce-scatter.4.cloned.1.call-start = ((), (), s32[]{:S(2)}) async-start(), calls=%async_computation.5 | async-start | bytes 10027008
  342.2 12.7 %copy-start.23 = (bf16[512,768]{1,0:T(8,128)(2,1)S(1)}, bf16[512,768]{1,0:T(8,128)(2,1)}, u32[]{:S(2)}) copy-start(bf16[512,768]{1,0:T(8,128)(2,1)} %copy-done.22) | copy-start | bytes 2359300
  347.3 25.6 %all-to-all-start.3 = ((bf16[16,32,2048]{2,1,0:T(8,128)(2,1)}), bf16[16,32,2048]{2,1,0:T(8,128)(2,1)S(1)}, u32[]{:S(2)}, u32[]{:S(2)}) async-start(bf16[16,32,2048]{2,1,0:T(8,128)(2,1)} %bitcast.68), calls=%async_computation.3 | async-start | bytes 4194304 | tf_op jit(solution)/shard_map/all_to_all | solution.py:80
  372.9 49.4 %all-to-all-start.1 = ((bf16[16,32,2048]{2,1,0:T(8,128)(2,1)}), bf16[16,32,2048]{2,1,0:T(8,128)(2,1)}, u32[]{:S(2)}, u32[]{:S(2)}) async-start(bf16[16,32,2048]{2,1,0:T(8,128)(2,1)} %bitcast.67), calls=%async_computation.1 | async-start | bytes 4194304 | tf_op jit(solution)/shard_map/all_to_all | solution.py:80
  384.2 106.0 %copy-start.1 = (bf16[1,2048,768]{2,1,0:T(8,128)(2,1)S(1)}, bf16[1,2048,768]{2,1,0:T(8,128)(2,1)}, u32[]{:S(2)}) copy-start(bf16[1,2048,768]{2,1,0:T(8,128)(2,1)} %param.11) | copy-start | bytes 9437188
  420.3 64.6 %collective-permute-start.16 = (bf16[128,2304]{0,1:T(8,128)(2,1)}, bf16[128,2304]{0,1:T(8,128)(2,1)}, u32[]{:S(2)}, u32[]{:S(2)}) collective-permute-start(bf16[128,2304]{0,1:T(8,128)(2,1)} %copy.26), channel_id=1, source_target_pairs={{0,0},{1,16},{2,32},{3,48},{4,64},{5,80},{6,96},{7,112},{8,128},{9... | collective-permute-start | bytes 1769480 | tf_op jit(solution)/shard_map/ppermute | solution.py:107
  (14 other events, 43.1 us)
Sparse Core Ops, SparseCore 0:
  337.4 80.7 reduce-scatter.3
